TPU v7x, 32 devices: a whole 2x2x4 slice. The times are simulated.
32 devices in a mesh: row: 4 (over y, x), col: 8 (over z, core).
Axes of the slice: x: 2, y: 2, z: 4, core: 2. Of those that a mesh axis runs over, the one named last changes fastest.
Arguments:
- fingerprints: bfloat16 [8192, 1024], P(('row', 'col')), as said below
- probes: bfloat16 [8192, 256], P(('row', 'col')), may hold values from -6 to 6
Outputs:
- image: float32 [8192, 256], P(('row', 'col'))
Inputs may be any that keep to these rules, and one draw needn't show every extreme that they name: `fingerprints`: every entry is positive.
All inputs are finite; a program needn't handle non-finite values.
Results may differ from a plain program's by a relative error of at most 0.0031.
Values may be sent and summed in bfloat16 or wider, within the bound.
A program may use at most 64 MiB of HBM per device.

v0:
```python
import math
import jax
import jax.numpy as jnp
from jax import lax
from jax.sharding import PartitionSpec as P


def squares(rows_now):
    values = rows_now.astype(jnp.float32)
    return jnp.sum(values * values, axis=1)


def tanimoto(first_rows, second_rows, first_sq, second_sq):
    inner = lax.dot_general(
        first_rows, second_rows, (((1,), (1,)), ((), ())), preferred_element_type=jnp.float32
    )
    kernel = inner / (first_sq[:, None] + second_sq[None, :] - inner)
    return kernel.astype(jnp.bfloat16)


def per_device(fingerprints, probes):
    molecules = fingerprints.shape[0] * lax.axis_size("row") * lax.axis_size("col")
    factor = 1.0 / math.sqrt(molecules)
    column_rows, column_probes = (
        lax.all_gather(fingerprints, "row", axis=0, tiled=True),
        lax.all_gather(probes, "row", axis=0, tiled=True),
    )
    column_sq = squares(column_rows)
    shard_rows = lax.all_gather(fingerprints, "col", axis=0, tiled=True)
    kernel = tanimoto(shard_rows, column_rows, squares(shard_rows), column_sq)
    partial_value = jnp.dot(kernel, column_probes, preferred_element_type=jnp.float32)
    owned = lax.psum_scatter(partial_value, "col", scatter_dimension=0, tiled=True)
    return owned * factor


def solution(mesh):
    return jax.shard_map(
        per_device,
        mesh=mesh,
        in_specs=(P(("row", "col"), None), P(("row", "col"), None)),
        out_specs=P(("row", "col"), None),
        check_vma=False,
    )
```

profile of v0, /device:TPU:0, one launch (start us, length us, event | category | flops | bytes accessed | tf_op | source)
XLA Modules:
  0.0 151.5 jit_solution(15270870452908466009)
XLA Ops:
  6.5 0.0 all-gather.5.cloned.1.call-start
  6.5 0.7 all-gather.5.cloned.1.call-update
  7.3 0.0 all-gather.3.cloned.1.call-start
  7.3 0.7 all-gather.3.cloned.1.call-update
  8.0 0.0 reduce-scatter.2.cloned.1.call-start
  8.1 11.8 %all_gather.11 = bf16[1024,256]{1,0:T(8,128)(2,1)S(1)} all-gather(bf16[256,256]{1,0:T(8,128)(2,1)} %param.3), channel_id=1, replica_groups=mesh['row'=4,'col'=8] {'row'}, dimensions={0}, use_global_device_ids=true | all-gather | bytes 655360 | tf_op jit(solution)/shard_map/all_gather | solution.py:26
  19.9 27.4 %all-gather.5.cloned.1.call-done = bf16[1024,1024]{1,0:T(8,128)(2,1)} async-done(((bf16[256,1024]{1,0:T(8,128)(2,1)}), bf16[1024,1024]{1,0:T(8,128)(2,1)}) %all-gather.5.cloned.1.call-update) | async-done | bytes 2097168 | tf_op jit(solution)/shard_map/all_gather | solution.py:25
  47.2 0.0 copy-start
  47.2 2.2 %multiply_reduce_fusion.1 = f32[1024]{0:T(1024)S(1)} fusion(bf16[1024,1024]{1,0:T(8,128)(2,1)} %all-gather.5.cloned.1.call-done), kind=kLoop, calls=%fused_computation.3 | loop fusion | flops 3144704 | bytes 2101248 | tf_op jit(solution)/shard_map/reduce_sum | solution.py:10
  49.5 46.6 %all-gather.3.cloned.1.call-done = bf16[2048,1024]{1,0:T(8,128)(2,1)} async-done(((bf16[256,1024]{1,0:T(8,128)(2,1)}), bf16[2048,1024]{1,0:T(8,128)(2,1)}) %all-gather.3.cloned.1.call-update) | async-done | bytes 4194320 | tf_op jit(solution)/shard_map/all_gather | solution.py:29
  96.0 3.1 %multiply_reduce_fusion = f32[2048]{0:T(1024)S(1)} fusion(bf16[2048,1024]{1,0:T(8,128)(2,1)} %all-gather.3.cloned.1.call-done), kind=kLoop, calls=%fused_computation.2 | loop fusion | flops 6289408 | bytes 4202496 | tf_op jit(solution)/shard_map/reduce_sum | solution.py:10
  99.1 0.0 copy-done
  99.1 9.4 %fusion.1 = f32[2048,256]{1,0:T(8,128)} fusion(bf16[1024,256]{1,0:T(8,128)(2,1)S(1)} %all_gather.11, f32[1024]{0:T(1024)S(1)} %multiply_reduce_fusion.1, f32[2048]{0:T(1024)S(1)} %multiply_reduce_fusion, bf16[2048,1024]{1,0:T(8,128)(2,1)} %all-gather.3.cloned.1.call-done, bf16[1024,1024]{1,0:T(8,128)(2,1)S(1)} %copy-done), kind=kOutput, calls=%fused_computation.4 | convolution fusion | flops 5377097728 | bytes 8925184 | tf_op jit(solution)/shard_map/dot_general | solution.py:31
  108.5 0.0 reduce-scatter.2.cloned.1.call-update
  108.5 34.8 %reduce-scatter.2.cloned.1.call-done = f32[256,256]{1,0:T(8,128)} async-done(((f32[2048,256]{1,0:T(8,128)}), f32[256,256]{1,0:T(8,128)}) %reduce-scatter.2.cloned.1.call-update) | async-done | bytes 262160 | tf_op jit(solution)/shard_map/reduce_scatter | solution.py:32
  143.3 1.7 %broadcast_multiply_fusion = f32[256,256]{1,0:T(8,128)} fusion(f32[256,256]{1,0:T(8,128)} %reduce-scatter.2.cloned.1.call-done), kind=kLoop, calls=%fused_computation.5 | loop fusion | flops 65536 | bytes 524288 | tf_op jit(solution)/shard_map/mul | solution.py:33
Async XLA Ops:
  6.5 40.7 %all-gather.5.cloned.1.call-start = ((), (), s32[]{:S(2)}) async-start(), calls=%async_computation.2 | async-start | bytes 2621440 | tf_op jit(solution)/shard_map/all_gather | solution.py:25
  7.3 88.8 %all-gather.3.cloned.1.call-start = ((), (), s32[]{:S(2)}) async-start(), calls=%async_computation.1 | async-start | bytes 4718592 | tf_op jit(solution)/shard_map/all_gather | solution.py:29
  8.0 135.3 %reduce-scatter.2.cloned.1.call-start = ((), (), s32[]{:S(2)}) async-start(), calls=%async_computation.3 | async-start | bytes 2359296 | tf_op jit(solution)/shard_map/reduce_scatter | solution.py:32
  47.2 51.9 %copy-start = (bf16[1024,1024]{1,0:T(8,128)(2,1)S(1)}, bf16[1024,1024]{1,0:T(8,128)(2,1)}, u32[]{:S(2)}) copy-start(bf16[1024,1024]{1,0:T(8,128)(2,1)} %all-gather.5.cloned.1.call-done) | copy-start | bytes 6291460
Sparse Core Ops, SparseCore 0:
  9.2 38.0 all-gather.4
  48.8 47.1 all-gather.2
  108.7 34.5 reduce-scatter.1
where the time goes:
time: 152 us; the launch traced here: 151 us
  waiting for transfers between devices  110 us (72%)
  between operations  13.1 us (9%)
  blocking collectives  11.8 us (8%)
  matrix products  9.4 us (6%)
  other arithmetic  6.96 us (5%)
    all_gather x1, waiting for transfers between devices, per_device(): shard_rows = lax.all_gather(fingerprints, 'col', axis=0, tiled=True)  46.6 us
    reduce_scatter x1, waiting for transfers between devices, per_device(): lax.psum_scatter(partial_value, 'col', scatter_dimension=0, tiled=True)  34.8 us
    all_gather x1, waiting for transfers between devices, per_device(): lax.all_gather(fingerprints, 'row', axis=0, tiled=True)  27.4 us
    all_gather x1, blocking collectives, per_device(): lax.all_gather(probes, 'row', axis=0, tiled=True)  11.8 us
    dot_general x1, matrix products, per_device(): jnp.dot(kernel, column_probes, preferred_element_type=jnp.float32)  9.4 us
    reduce_sum x2, other arithmetic, squares(): return jnp.sum(values * values, axis=1)  5.29 us
  transfers between devices with their start and end apart: 3, of which 3 were waited for; matrix products, arithmetic and copies ran while one was open for 1% of the time, Pallas kernels for 0%

commit v1 on v0

--- a/solution.py
+++ b/solution.py
@@ -3,6 +3,18 @@
 import jax.numpy as jnp
 from jax import lax
 from jax.sharding import PartitionSpec as P
+
+
+def gather_by_bits(value, axis, dim):
+    ways, here = (lax.axis_size(axis), lax.axis_index(axis))
+    grown, reach = (value, 1)
+    while reach < ways:
+        theirs = lax.ppermute(grown, axis, [(d, d ^ reach) for d in range(ways)])
+        mine_first = jnp.concatenate([grown, theirs], axis=dim)
+        theirs_first = jnp.concatenate([theirs, grown], axis=dim)
+        grown = jnp.where(here & reach == 0, mine_first, theirs_first)
+        reach = 2 * reach
+    return grown
 
 
 def squares(rows_now):
@@ -22,7 +34,7 @@
     molecules = fingerprints.shape[0] * lax.axis_size("row") * lax.axis_size("col")
     factor = 1.0 / math.sqrt(molecules)
     column_rows, column_probes = (
-        lax.all_gather(fingerprints, "row", axis=0, tiled=True),
+        gather_by_bits(fingerprints, "row", 0),
         lax.all_gather(probes, "row", axis=0, tiled=True),
     )
     column_sq = squares(column_rows)

time: 152 us -> 115 us (0.76)
  waiting for transfers between devices: 110 us -> 51.3 us
  blocking collectives: 11.8 us -> 28.4 us
  starting transfers between devices: 0.08 us -> 4.88 us
    all_gather x1, waiting for transfers between devices: 46.6 us -> 3.76 us  [per_device(): shard_rows = lax.all_gather(fingerprints, 'col', axis=0, tiled=True)]
    all_gather x1 -> x0, waiting for transfers between devices: 27.4 us -> none  [per_device(): lax.all_gather(fingerprints, 'row', axis=0, tiled=True)]
    all_gather x1, blocking collectives: 11.8 us -> 28.4 us  [per_device(): lax.all_gather(probes, 'row', axis=0, tiled=True)]
    ppermute x0 -> x2, waiting for transfers between devices: none -> 12.1 us  [gather_by_bits(): theirs = lax.ppermute(grown, axis, [(d, d ^ reach) for d in range(ways)])]
    ppermute x0 -> x2, starting transfers between devices: none -> 4.84 us  [gather_by_bits(): theirs = lax.ppermute(grown, axis, [(d, d ^ reach) for d in range(ways)])]
    select_n x0 -> x1, other arithmetic: none -> 1.62 us  [gather_by_bits(): grown = jnp.where(here & reach == 0, mine_first, theirs_first)]
  transfers between devices with their start and end apart: 3 -> 4, of which waited for: 3 -> 3; matrix products, arithmetic and copies ran while one was open for 1% -> 2% of each run, Pallas kernels for 0% -> 0%
where the time goes in v1:
time: 115 us
  waiting for transfers between devices  51.3 us (45%)
  blocking collectives  28.4 us (25%)
  between operations  13.4 us (12%)
  matrix products  9.53 us (8%)
  other arithmetic  7.12 us (6%)
  starting transfers between devices  4.88 us (4%)
    reduce_scatter x1, waiting for transfers between devices, per_device(): lax.psum_scatter(partial_value, 'col', scatter_dimension=0, tiled=True)  34.7 us
    all_gather x1, blocking collectives, per_device(): lax.all_gather(probes, 'row', axis=0, tiled=True)  28.4 us
    ppermute x2, waiting for transfers between devices, gather_by_bits(): theirs = lax.ppermute(grown, axis, [(d, d ^ reach) for d in range(ways)])  12.1 us
    dot_general x1, matrix products, per_device(): jnp.dot(kernel, column_probes, preferred_element_type=jnp.float32)  9.53 us
    ppermute x2, starting transfers between devices, gather_by_bits(): theirs = lax.ppermute(grown, axis, [(d, d ^ reach) for d in range(ways)])  4.84 us
    reduce_sum x2, other arithmetic, squares(): return jnp.sum(values * values, axis=1)  3.82 us
    all_gather x1, waiting for transfers between devices, per_device(): shard_rows = lax.all_gather(fingerprints, 'col', axis=0, tiled=True)  3.76 us
  transfers between devices with their start and end apart: 4, of which 3 were waited for; matrix products, arithmetic and copies ran while one was open for 2% of the time, Pallas kernels for 0%

profile of v1, /device:TPU:0, one launch (start us, length us, event | category | flops | bytes accessed | tf_op | source)
XLA Modules:
  0.0 114.7 jit_solution(3704957874694984958)
XLA Ops:
  6.5 0.0 all-gather.2.cloned.1.call-start
  6.5 0.7 all-gather.2.cloned.1.call-update
  7.3 0.0 reduce-scatter.2.cloned.1.call-start
  7.3 3.0 %collective-permute-start = (bf16[256,1024]{1,0:T(8,128)(2,1)}, bf16[256,1024]{1,0:T(8,128)(2,1)S(1)}, u32[]{:S(2)}, u32[]{:S(2)}) collective-permute-start(bf16[256,1024]{1,0:T(8,128)(2,1)} %param.2), channel_id=1, source_target_pairs={{0,8},{8,0},{16,24},{24,16},{1,9},{9,1},{17,25},{25,17},{2,10},{10... | collective-permute-start | bytes 1572872 | tf_op jit(solution)/shard_map/ppermute | solution.py:12
  10.3 12.1 %collective-permute-done = bf16[256,1024]{1,0:T(8,128)(2,1)S(1)} collective-permute-done((bf16[256,1024]{1,0:T(8,128)(2,1)}, bf16[256,1024]{1,0:T(8,128)(2,1)S(1)}, u32[]{:S(2)}, u32[]{:S(2)}) %collective-permute-start) | collective-permute-done | bytes 524320 | tf_op jit(solution)/shard_map/ppermute | solution.py:12
  22.4 1.6 %maximum_select_fusion.1 = bf16[512,1024]{1,0:T(8,128)(2,1)S(1)} fusion(bf16[256,1024]{1,0:T(8,128)(2,1)S(1)} %collective-permute-done, bf16[256,1024]{1,0:T(8,128)(2,1)} %param.2, pred[]{:T(512)S(6)} %eq.7), kind=kLoop, calls=%fused_computation.6 | loop fusion | flops 4718592 | bytes 2097153 | tf_op jit(solution)/shard_map/jit(_where)/select_n | solution.py:15
  24.1 1.8 %collective-permute-start.1 = (bf16[512,1024]{1,0:T(8,128)(2,1)S(1)}, bf16[512,1024]{1,0:T(8,128)(2,1)S(1)}, u32[]{:S(2)}, u32[]{:S(2)}) collective-permute-start(bf16[512,1024]{1,0:T(8,128)(2,1)S(1)} %maximum_select_fusion.1), channel_id=1, source_target_pairs={{0,16},{8,24},{16,0},{24,8},{1,17},{9,25},{17,1},{25,9},{2,18},{10... | collective-permute-start | bytes 3145736 | tf_op jit(solution)/shard_map/ppermute | solution.py:12
  25.9 28.4 %all_gather.7 = bf16[1024,256]{1,0:T(8,128)(2,1)S(1)} all-gather(bf16[256,256]{1,0:T(8,128)(2,1)} %param.3), channel_id=1, replica_groups=mesh['row'=4,'col'=8] {'row'}, dimensions={0}, use_global_device_ids=true | all-gather | bytes 655360 | tf_op jit(solution)/shard_map/all_gather | solution.py:38
  54.3 0.0 collective-permute-done.1
  54.3 0.7 multiply_reduce_fusion.1
  55.1 3.8 %all-gather.2.cloned.1.call-done = bf16[2048,1024]{1,0:T(8,128)(2,1)} async-done(((bf16[256,1024]{1,0:T(8,128)(2,1)}), bf16[2048,1024]{1,0:T(8,128)(2,1)}) %all-gather.2.cloned.1.call-update) | async-done | bytes 4194320 | tf_op jit(solution)/shard_map/all_gather | solution.py:41
  58.8 3.1 %multiply_reduce_fusion = f32[2048]{0:T(1024)S(1)} fusion(bf16[2048,1024]{1,0:T(8,128)(2,1)} %all-gather.2.cloned.1.call-done), kind=kLoop, calls=%fused_computation.2 | loop fusion | flops 6289408 | bytes 4202496 | tf_op jit(solution)/shard_map/reduce_sum | solution.py:22
  61.9 9.5 %fusion.1 = f32[2048,256]{1,0:T(8,128)} fusion(bf16[1024,256]{1,0:T(8,128)(2,1)S(1)} %all_gather.7, bf16[2048,1024]{1,0:T(8,128)(2,1)} %all-gather.2.cloned.1.call-done, f32[1024]{0:T(1024)S(1)} %multiply_reduce_fusion.1, f32[2048]{0:T(1024)S(1)} %multiply_reduce_fusion, bf16[512,1024]{1,0:T(8,128)(2,1)S(1)} %collective-permute-done.1, ...), kind=kOutput, calls=%fused_computation.5 | convolution fusion | flops 5386534912 | bytes 8925185 | tf_op jit(solution)/shard_map/dot_general | solution.py:43
  71.4 0.0 reduce-scatter.2.cloned.1.call-update
  71.5 34.7 %reduce-scatter.2.cloned.1.call-done = f32[256,256]{1,0:T(8,128)} async-done(((f32[2048,256]{1,0:T(8,128)}), f32[256,256]{1,0:T(8,128)}) %reduce-scatter.2.cloned.1.call-update) | async-done | bytes 262160 | tf_op jit(solution)/shard_map/reduce_scatter | solution.py:44
  106.1 1.7 %broadcast_multiply_fusion = f32[256,256]{1,0:T(8,128)} fusion(f32[256,256]{1,0:T(8,128)} %reduce-scatter.2.cloned.1.call-done), kind=kLoop, calls=%fused_computation.7 | loop fusion | flops 65536 | bytes 524288 | tf_op jit(solution)/shard_map/mul | solution.py:45
Async XLA Ops:
  6.5 52.3 %all-gather.2.cloned.1.call-start = ((), (), s32[]{:S(2)}) async-start(), calls=%async_computation.1 | async-start | bytes 4718592 | tf_op jit(solution)/shard_map/all_gather | solution.py:41
  7.3 98.9 %reduce-scatter.2.cloned.1.call-start = ((), (), s32[]{:S(2)}) async-start(), calls=%async_computation.2 | async-start | bytes 2359296 | tf_op jit(solution)/shard_map/reduce_scatter | solution.py:44
  7.3 15.1 %collective-permute-start = (bf16[256,1024]{1,0:T(8,128)(2,1)}, bf16[256,1024]{1,0:T(8,128)(2,1)S(1)}, u32[]{:S(2)}, u32[]{:S(2)}) collective-permute-start(bf16[256,1024]{1,0:T(8,128)(2,1)} %param.2), channel_id=1, source_target_pairs={{0,8},{8,0},{16,24},{24,16},{1,9},{9,1},{17,25},{25,17},{2,10},{10... | collective-permute-start | bytes 1572872 | tf_op jit(solution)/shard_map/ppermute | solution.py:12
  24.1 30.3 %collective-permute-start.1 = (bf16[512,1024]{1,0:T(8,128)(2,1)S(1)}, bf16[512,1024]{1,0:T(8,128)(2,1)S(1)}, u32[]{:S(2)}, u32[]{:S(2)}) collective-permute-start(bf16[512,1024]{1,0:T(8,128)(2,1)S(1)} %maximum_select_fusion.1), channel_id=1, source_target_pairs={{0,16},{8,24},{16,0},{24,8},{1,17},{9,25},{17,1},{25,9},{2,18},{10... | collective-permute-start | bytes 3145736 | tf_op jit(solution)/shard_map/ppermute | solution.py:12
Sparse Core Ops, SparseCore 0:
  9.0 49.8 all-gather.1
  71.6 34.5 reduce-scatter.1
